TPU v7x, 32 devices: a whole 2x2x4 slice. The times are simulated.
32 devices in a mesh: grp: 2 (over x), chan: 16 (over z, y, core).
Axes of the slice: x: 2, y: 2, z: 4, core: 2. Of those that a mesh axis runs over, the one named last changes fastest.
Arguments:
- samples: bfloat16 [32, 16, 256, 1024], P(('grp', 'chan')), parts along dimension 0, may hold values from -6 to 6
- fir: float32 [16, 1024], replicated, may hold values from -1.5 to 1.5
- chan_assign: int32 [256], replicated, may hold values from 0 to 511, as said below
- input_order: int32 [1024], replicated, may hold values from 0 to 1023, each once
Outputs:
- vis: bfloat16 [512, 1024, 1024], P(('grp', 'chan')), parts along dimension 0
There are 2 independent parts, one for each index of `grp`. A program takes and returns all parts, laid end to end along the dimension named above; an argument that names none is the same for every part. Nothing has to cross between parts.
Inputs may be any that keep to these rules, and one draw needn't show every extreme that they name: `chan_assign`: distinct transform bins; bin 0 and bin 1024 // 2 - 1 are always among them. `input_order`: each input number once.
All inputs are finite; a program needn't handle non-finite values.
Results may differ from a plain program's by a relative error of at most 0.0074.
Values may be sent and summed in bfloat16 or wider, within the bound.
A program may use at most 256 MiB of HBM per device.

v0:
```python
import math

import jax
import jax.numpy as jnp
from jax import lax
from jax.sharding import PartitionSpec as P

QUART = 4


def shifted(value, axis, steps):
    count = lax.axis_size(axis)
    initial, last = (max(0, -steps), min(count, count - steps))
    return lax.ppermute(value, axis, [(source, source + steps) for source in range(initial, last)])


def make_table(chan_assign, frame_len):
    samples_index = jnp.arange(frame_len, dtype=jnp.int32)
    phase_index = chan_assign[:, None] * samples_index[None, :] % frame_len
    angles = phase_index.astype(jnp.float32) * (2.0 * math.pi / frame_len)
    norm_scale = 1.0 / math.sqrt(frame_len)
    return jnp.stack([jnp.cos(angles) * norm_scale, -jnp.sin(angles) * norm_scale]).astype(
        jnp.bfloat16
    )


def on_device(samples, fir, chan_assign, input_order):
    own_frames = samples[0]
    frames_quarter, slots_dev, frame_len = own_frames.shape
    taps_count = fir.shape[0]
    chan_count = lax.axis_size("chan")
    group_count = chan_count // QUART
    history_len = taps_count - 1
    lead_len = min(frames_quarter, history_len)
    tail_frames = own_frames[frames_quarter - lead_len :]
    pieces = shifted(tail_frames, "chan", 1 * group_count)
    extended = jnp.concatenate([pieces, own_frames], axis=0)
    dft_table = make_table(chan_assign, frame_len)
    chan_total = chan_assign.shape[0]
    chan_dev = chan_total // chan_count
    inputs_all = input_order.shape[0]
    inverse = jnp.argsort(input_order)
    spectra_total = QUART * frames_quarter
    accum = jnp.zeros((frames_quarter, slots_dev, frame_len), jnp.float32)
    for tap_index in range(taps_count):
        begin = 0 + history_len - tap_index
        accum = accum + fir[tap_index][None, None, :] * extended[
            begin : begin + frames_quarter
        ].astype(jnp.float32)
    filtered = accum.astype(jnp.bfloat16)
    spectra = jnp.einsum("pcn,fin->cfpi", dft_table, filtered, preferred_element_type=jnp.float32)
    spectra = spectra.astype(jnp.bfloat16).reshape(
        chan_count, chan_dev, frames_quarter, 2, slots_dev
    )
    received = lax.all_to_all(spectra, "chan", split_axis=0, concat_axis=4, tiled=True)
    items = received.shape[1]
    row_count = received.shape[2]
    split_parts = received.reshape(items, row_count, 2, QUART, inputs_all)
    ordered = jnp.take(split_parts, inverse, axis=4)
    stacked = ordered.reshape(items, row_count * 2 * QUART, inputs_all)
    real_rows = ordered[:, :, 0].reshape(items, row_count * QUART, inputs_all)
    imag_rows = ordered[:, :, 1].reshape(items, row_count * QUART, inputs_all)
    auto_sum = jnp.einsum("kra,krb->kab", stacked, stacked, preferred_element_type=jnp.float32)
    cross_sum = jnp.einsum("kra,krb->kab", real_rows, imag_rows, preferred_element_type=jnp.float32)
    row_index = lax.broadcasted_iota(jnp.int32, (inputs_all, inputs_all), 0)
    col_index = lax.broadcasted_iota(jnp.int32, (inputs_all, inputs_all), 1)
    upper_mask = (row_index <= col_index)[None, :, :]
    packed = (
        jnp.where(upper_mask, auto_sum, cross_sum - jnp.swapaxes(cross_sum, 1, 2)) / spectra_total
    )
    return packed.astype(jnp.bfloat16)


def solution(mesh):
    in_specs = (P(("grp", "chan"), None, None, None), P(), P(), P())
    out_specs = P(("grp", "chan"), None, None)
    return jax.shard_map(
        on_device, mesh=mesh, in_specs=in_specs, out_specs=out_specs, check_vma=False
    )
```

profile of v0, /device:TPU:8, one launch (start us, length us, event | category | flops | bytes accessed | tf_op | source)
XLA Modules:
  0.0 706.9 jit_solution(15074221744417982181)
XLA Ops:
  0.0 4.2 slice_bitcast_fusion
  4.2 3.5 collective-permute-start
  7.7 1.3 fusion.34
  9.0 5.6 multiply_convert_fusion.1
  14.6 162.5 %collective-permute-done = bf16[15,256,1024]{2,1,0:T(8,128)(2,1)} collective-permute-done((bf16[15,256,1024]{2,1,0:T(8,128)(2,1)S(1)}, bf16[15,256,1024]{2,1,0:T(8,128)(2,1)}, u32[]{:S(2)}, u32[]{:S(2)}) %collective-permute-start) | collective-permute-done | bytes 7864352 | tf_op jit(solution)/shard_map/ppermute | solution.py:14
  177.1 58.6 %fusion.41 = bf16[16,256,1024,1]{2,1,3,0:T(8,128)(2,1)} fusion(bf16[16,256,1024]{2,1,0:T(8,128)(2,1)} %bitcast.64, bf16[15,256,1024]{2,1,0:T(8,128)(2,1)} %collective-permute-done, f32[1024]{0:T(1024)S(1)} %bitcast.80, f32[1024]{0:T(1024)S(1)} %bitcast.81, f32[1024]{0:T(1024)S(1)} %bitcast.67, f32[1024]{0:T(1024)S(1)} %bitcast.68, ...), kind=kLoop, calls=%fused_computation.51.clone.clone.clone.2 | loop fusion | flops 264241152 | bytes 24707072 | tf_op jit(solution)/shard_map/pcn,fin->cfpi/dot_general | solution.py:51
  235.7 8.2 %fusion.20 = bf16[16,256,2,256]{1,3,2,0:T(8,128)(2,1)S(1)} fusion(bf16[1,256,1024]{2,1,0:T(8,128)(2,1)S(1)} %get-tuple-element.26, bf16[1,256,1024]{2,1,0:T(8,128)(2,1)S(1)} %get-tuple-element.25, bf16[16,256,1024,1]{2,1,3,0:T(8,128)(2,1)} %fusion.41), kind=kOutput, calls=%fused_computation.56 | convolution fusion | flops 4299161600 | bytes 13631488 | tf_op jit(solution)/shard_map/pcn,fin->cfpi/dot_general | solution.py:51
  243.9 0.0 copy-start
  243.9 6.5 copy.16
  250.4 6.3 all-to-all-start
  256.7 0.0 copy-done
  256.7 4.4 sort.17
  261.1 0.3 iota_compare_fusion
  261.4 86.1 %all-to-all-done = bf16[16,16,16,2,256]{4,3,2,1,0:T(2,128)(2,1)} async-done(((bf16[16,16,16,2,256]{4,3,2,1,0:T(2,128)(2,1)}), bf16[16,16,16,2,256]{4,3,2,1,0:T(2,128)(2,1)}, u32[]{:S(2)}, u32[]{:S(2)}) %all-to-all-start) | async-done | bytes 4194336 | tf_op jit(solution)/shard_map/all_to_all | solution.py:55
  347.5 32.4 %copy.26 = bf16[1,16,16,2,16,256]{2,1,5,4,3,0:T(8,128)(2,1)} copy(bf16[1,16,16,2,16,256]{5,3,2,1,4,0:T(2,128)(2,1)} %bitcast.24) | data formatting | bytes 8388608 | tf_op jit(solution)/shard_map/reshape | solution.py:58
  379.9 36.7 %gather_fusion = bf16[1024,16,16,2,4]{2,1,4,3,0:T(8,128)(2,1)} fusion(bf16[16,16,2,4,1024]{1,0,4,3,2:T(8,128)(2,1)} %bitcast.63, s32[1024]{0:T(1024)S(1)} %fusion.31), kind=kCustom, calls=%fused_computation | custom fusion | bytes 8392704 | tf_op jit(solution)/shard_map/jit(_take)/gather | solution.py:59
  416.6 35.7 %copy.19 = bf16[16,16,2,4,1024]{4,0,3,2,1:T(8,128)(2,1)} copy(bf16[16,16,2,4,1024]{1,0,3,2,4:T(8,128)(2,1)} %bitcast.62) | data formatting | bytes 8388608 | tf_op jit(solution)/shard_map/jit(_take)/gather | solution.py:59
  452.3 22.7 %broadcast_select_fusion = bf16[16,16,2,4,1024]{1,0,3,2,4:T(8,128)(2,1)} fusion(pred[1024]{0:T(1024)(128)(4,1)S(1)} %compare_and_fusion, bf16[1024,16,16,2,4]{2,1,4,3,0:T(8,128)(2,1)} %gather_fusion), kind=kLoop, calls=%fused_computation.33 | loop fusion | flops 2097152 | bytes 8389632 | tf_op jit(solution)/shard_map/jit(_take)/select_n | solution.py:59
  475.0 4.5 bitcast_select_fusion
  479.5 25.2 %fusion.33 = (bf16[16,16,1,4,1024]{1,0,3,2,4:T(8,128)(2,1)}, bf16[16,16,1,4,1024]{1,0,3,2,4:T(8,128)(2,1)}) fusion(bf16[16,16,2,4,1024]{1,0,3,2,4:T(8,128)(2,1)} %broadcast_select_fusion), kind=kLoop, calls=%fused_computation.75 | loop fusion | bytes 8388608 | tf_op jit(solution)/shard_map/slice | solution.py:62
  504.7 21.9 %copy.23 = bf16[16,16,1,4,1024]{4,3,1,0,2:T(4,128)(2,1)} copy(bf16[16,16,1,4,1024]{1,0,3,2,4:T(8,128)(2,1)} %get-tuple-element.7) | data formatting | bytes 4194304 | tf_op jit(solution)/shard_map/slice | solution.py:62
  526.6 2.5 reshape_squeeze.7
  529.2 21.9 %copy.22 = bf16[16,16,1,4,1024]{4,3,1,0,2:T(4,128)(2,1)} copy(bf16[16,16,1,4,1024]{1,0,3,2,4:T(8,128)(2,1)} %get-tuple-element.8) | data formatting | bytes 4194304 | tf_op jit(solution)/shard_map/slice | solution.py:61
  551.1 4.0 reshape_squeeze.6
  555.0 24.8 %fusion.35 = f32[16,1024,1024]{2,1,0:T(8,128)} fusion(bf16[16,64,1024]{2,1,0:T(8,128)(2,1)} %reshape_squeeze.6, bf16[16,64,1024]{2,1,0:T(8,128)(2,1)S(1)} %reshape_squeeze.7), kind=kOutput, calls=%fused_computation.77 | convolution fusion | flops 2147483648 | bytes 71303168 | tf_op jit(solution)/shard_map/kra,krb->kab/dot_general | solution.py:64
  579.8 62.8 %copy.24 = f32[16,1024,1024]{1,2,0:T(8,128)} copy(f32[16,1024,1024]{2,1,0:T(8,128)} %fusion.35) | data formatting | bytes 134217728 | tf_op jit(solution)/shard_map/kra,krb->kab/dot_general | solution.py:64
  642.7 64.2 %fusion.2 = bf16[16,1024,1024]{2,1,0:T(8,128)(2,1)} fusion(f32[16,1024,1024]{2,1,0:T(8,128)} %fusion.35, f32[16,1024,1024]{1,2,0:T(8,128)} %copy.24, pred[1024,1024]{1,0:T(8,128)(4,1)S(1)} %iota_compare_fusion, bf16[16,128,1024]{2,0,1:T(8,128)(2,1)} %bitcast_select_fusion), kind=kOutput, calls=%fused_computation.4 | convolution fusion | flops 4362076160 | bytes 173015040 | tf_op jit(solution)/shard_map/kra,krb->kab/dot_general | solution.py:63
  (3 shorter events, 0.0 us)
Async XLA Ops:
  4.2 173.0 %collective-permute-start = (bf16[15,256,1024]{2,1,0:T(8,128)(2,1)S(1)}, bf16[15,256,1024]{2,1,0:T(8,128)(2,1)}, u32[]{:S(2)}, u32[]{:S(2)}) collective-permute-start(bf16[15,256,1024]{2,1,0:T(8,128)(2,1)S(1)} %slice_bitcast_fusion), channel_id=1, source_target_pairs={{0,4},{1,5},{2,6},{3,7},{4,8},{5,9},{6,10},{7,11},{8,12},{9,13},{1... | collective-permute-start | bytes 23592968 | tf_op jit(solution)/shard_map/ppermute | solution.py:14
  243.9 12.8 %copy-start = (s32[1024]{0:T(1024)S(1)}, s32[1024]{0:T(1024)}, u32[]{:S(2)}) copy-start(s32[1024]{0:T(1024)} %param.7) | copy-start | bytes 12292
  250.4 97.1 %all-to-all-start = ((bf16[16,16,16,2,256]{4,3,2,1,0:T(2,128)(2,1)}), bf16[16,16,16,2,256]{4,3,2,1,0:T(2,128)(2,1)}, u32[]{:S(2)}, u32[]{:S(2)}) async-start(bf16[16,16,16,2,256]{4,3,2,1,0:T(2,128)(2,1)} %copy.16), calls=%async_computation | async-start | bytes 8388608 | tf_op jit(solution)/shard_map/all_to_all | solution.py:55
where the time goes:
time: 714 us; the launch traced here: 707 us
  local copies, waits for them, and re-layouts  255 us (36%)
  waiting for transfers between devices  249 us (35%)
  matrix products  97.2 us (14%)
  other arithmetic  96.1 us (13%)
  starting transfers between devices  9.78 us (1%)
    ppermute x1, waiting for transfers between devices, shifted(): lax.ppermute(value, axis, [(source, source + steps) for source in range(i...  163 us
    all_to_all x1, waiting for transfers between devices, on_device(): lax.all_to_all(spectra, 'chan', split_axis=0, concat_axis=4, tiled=True)  86.1 us
    gather x2, local copies, waits for them, and re-layouts, on_device(): ordered = jnp.take(split_parts, inverse, axis=4)  72.4 us
    dot_general x1, matrix products, on_device(): jnp.einsum('kra,krb->kab', stacked, stacked, preferred_element_type=jnp.f...  64.2 us
    dot_general x1, local copies, waits for them, and re-layouts, on_device(): jnp.einsum('kra,krb->kab', real_rows, imag_rows, preferred_element_type=j...  62.8 us
    dot_general x1, other arithmetic, on_device(): jnp.einsum('pcn,fin->cfpi', dft_table, filtered, preferred_element_type=j...  58.6 us
    slice x2, local copies, waits for them, and re-layouts, on_device(): imag_rows = ordered[:, :, 1].reshape(items, row_count * QUART, inputs_all)  47.1 us
    reshape x1, local copies, waits for them, and re-layouts, on_device(): split_parts = received.reshape(items, row_count, 2, QUART, inputs_all)  32.4 us
  transfers between devices with their start and end apart: 2, of which 2 were waited for; matrix products, arithmetic and copies ran while one was open for 2% of the time, Pallas kernels for 0%

commit v1 on v0

--- a/solution.py
+++ b/solution.py
@@ -3,9 +3,12 @@
 import jax
 import jax.numpy as jnp
 from jax import lax
+from jax.experimental import pallas as pl
+from jax.experimental.pallas import tpu as pltpu
 from jax.sharding import PartitionSpec as P
 
 QUART = 4
+VMEM = 60 * 1024 * 1024
 
 
 def shifted(value, axis, steps):
@@ -24,7 +27,147 @@
     )
 
 
-def on_device(samples, fir, chan_assign, input_order):
+def spectra_kernel(x_ref, fir_ref, dft_ref, out_ref, filt):
+    frames, slots, frame_len = x_ref.shape
+    taps = fir_ref.shape[0]
+    dests, outs, _, chan_dev, _ = out_ref.shape
+    slot_tiles = slots // 16
+
+    @pl.loop(0, slot_tiles * (frame_len // 128))
+    def _(step):
+        rows = pl.ds(pl.multiple_of(lax.rem(step, slot_tiles) * 16, 16), 16)
+        cols = pl.ds(pl.multiple_of(lax.div(step, slot_tiles) * 128, 128), 128)
+        x = [x_ref[f, rows, cols].astype(jnp.float32) for f in range(frames)]
+        fir = [fir_ref[t : t + 1, cols] for t in range(taps)]
+        for o in range(outs):
+            accum = None
+            for t in range(taps):
+                if 0 <= o - t < frames:
+                    term = fir[t] * x[o - t]
+                    accum = term if accum is None else accum + term
+            filt[o, rows, cols] = accum.astype(jnp.bfloat16)
+
+    @pl.loop(0, outs)
+    def _(o):
+        result = lax.dot_general(
+            dft_ref[...],
+            filt[o],
+            (((1,), (1,)), ((), ())),
+            preferred_element_type=jnp.float32,
+        ).astype(jnp.bfloat16)
+        for p in range(2):
+            for d in range(dests):
+                begin = (p * dests + d) * chan_dev
+                out_ref[d, o, p] = result[begin : begin + chan_dev]
+
+
+def form_spectra(own_frames, fir, dft_table, dests):
+    frames, slots, frame_len = own_frames.shape
+    outs = frames + fir.shape[0] - 1
+    chan_dev = dft_table.shape[1] // dests
+    return pl.pallas_call(
+        spectra_kernel,
+        out_shape=jax.ShapeDtypeStruct((dests, outs, 2, chan_dev, slots), jnp.bfloat16),
+        in_specs=[pl.BlockSpec(memory_space=pltpu.VMEM)] * 3,
+        out_specs=pl.BlockSpec(memory_space=pltpu.VMEM),
+        scratch_shapes=[pltpu.VMEM((outs, slots, frame_len), jnp.bfloat16)],
+        compiler_params=pltpu.CompilerParams(vmem_limit_bytes=VMEM),
+        name="form_spectra",
+    )(own_frames, fir, dft_table.reshape(-1, frame_len))
+
+
+def correlate_kernel(spec_ref, order_ref, out_ref, gathered, select, ordered):
+    sources, outs, _, chan_dev, slots = spec_ref.shape
+    groups = sources // QUART
+    inputs = order_ref.shape[0]
+    rows_total = gathered.shape[0] // chan_dev
+    frames = rows_total // (2 * QUART)
+    lead = outs - frames
+    spectra_total = QUART * frames
+
+    @pl.when(pl.program_id(0) == 0)
+    def _():
+        for p in range(2):
+            for q in range(QUART):
+                base = (p * QUART + q) * frames * chan_dev
+                for g in range(groups):
+                    cols = slice(g * slots, (g + 1) * slots)
+                    source = q * groups + g
+                    for f in range(frames):
+                        value = spec_ref[source, f, p]
+                        if q > 0 and f < lead:
+                            value = (
+                                value.astype(jnp.float32)
+                                + spec_ref[source - groups, frames + f, p].astype(jnp.float32)
+                            ).astype(jnp.bfloat16)
+                        gathered[base + f * chan_dev : base + (f + 1) * chan_dev, cols] = value
+        for begin in range(0, inputs, 128):
+            names = lax.broadcasted_iota(jnp.int32, (128, inputs), 1)
+            hit = names == order_ref[begin : begin + 128, :]
+            select[begin : begin + 128, :] = hit.astype(jnp.float32).astype(jnp.bfloat16)
+
+        @pl.loop(0, gathered.shape[0] // 256)
+        def _(step):
+            rows = pl.ds(pl.multiple_of(step * 256, 256), 256)
+            result = jnp.dot(gathered[rows, :], select[...], preferred_element_type=jnp.float32)
+            for k in range(inputs // 128):
+                ordered[k, rows, :] = result[:, k * 128 : (k + 1) * 128]
+
+    own_rows = pl.ds(pl.program_id(0), rows_total, stride=chan_dev)
+    both = jnp.concatenate([ordered[k, own_rows, :] for k in range(inputs // 128)], axis=1)
+    half = rows_total // 2
+    turned = both.T.astype(jnp.bfloat16)
+    auto_side = both.astype(jnp.bfloat16)
+    cross_side = jnp.concatenate([both[half:], -both[:half]], axis=0).astype(jnp.bfloat16)
+    tile = 256
+    scale = 1.0 / spectra_total
+    upper = lax.broadcasted_iota(jnp.int32, (tile, tile), 0) <= lax.broadcasted_iota(
+        jnp.int32, (tile, tile), 1
+    )
+    for begin in range(0, inputs, tile):
+        left = turned[begin : begin + tile]
+        for other in range(0, inputs, tile):
+            cols = slice(other, other + tile)
+            value = None
+            if other >= begin:
+                value = jnp.dot(left, auto_side[:, cols], preferred_element_type=jnp.float32)
+            if other <= begin:
+                cross = jnp.dot(left, cross_side[:, cols], preferred_element_type=jnp.float32)
+                value = cross if value is None else jnp.where(upper, value, cross)
+            out_ref[0, begin : begin + tile, cols] = (value * scale).astype(jnp.bfloat16)
+
+
+def correlate(received, input_order, frames):
+    sources, outs, _, chan_dev, slots = received.shape
+    inputs = input_order.shape[0]
+    rows = 2 * QUART * frames * chan_dev
+    return pl.pallas_call(
+        correlate_kernel,
+        grid=(chan_dev,),
+        out_shape=jax.ShapeDtypeStruct((chan_dev, inputs, inputs), jnp.bfloat16),
+        in_specs=[pl.BlockSpec(memory_space=pltpu.VMEM)] * 2,
+        out_specs=pl.BlockSpec((1, inputs, inputs), lambda c: (c, 0, 0)),
+        scratch_shapes=[
+            pltpu.VMEM((rows, inputs), jnp.bfloat16),
+            pltpu.VMEM((inputs, inputs), jnp.bfloat16),
+            pltpu.VMEM((inputs // 128, rows, 128), jnp.float32),
+        ],
+        compiler_params=pltpu.CompilerParams(vmem_limit_bytes=VMEM),
+        name="correlate",
+    )(received, input_order[:, None])
+
+
+def by_kernels(samples, fir, chan_assign, input_order):
+    own_frames = samples[0]
+    frames, _, frame_len = own_frames.shape
+    chan_count = lax.axis_size("chan")
+    dft_table = make_table(chan_assign, frame_len)
+    spectra = form_spectra(own_frames, fir, dft_table, chan_count)
+    received = lax.all_to_all(spectra, "chan", split_axis=0, concat_axis=0, tiled=True)
+    return correlate(received, input_order, frames)
+
+
+def plain(samples, fir, chan_assign, input_order):
     own_frames = samples[0]
     frames_quarter, slots_dev, frame_len = own_frames.shape
     taps_count = fir.shape[0]
@@ -36,10 +179,8 @@
     pieces = shifted(tail_frames, "chan", 1 * group_count)
     extended = jnp.concatenate([pieces, own_frames], axis=0)
     dft_table = make_table(chan_assign, frame_len)
-    chan_total = chan_assign.shape[0]
-    chan_dev = chan_total // chan_count
+    chan_dev = chan_assign.shape[0] // chan_count
     inputs_all = input_order.shape[0]
-    inverse = jnp.argsort(input_order)
     spectra_total = QUART * frames_quarter
     accum = jnp.zeros((frames_quarter, slots_dev, frame_len), jnp.float32)
     for tap_index in range(taps_count):
@@ -55,8 +196,12 @@
     received = lax.all_to_all(spectra, "chan", split_axis=0, concat_axis=4, tiled=True)
     items = received.shape[1]
     row_count = received.shape[2]
-    split_parts = received.reshape(items, row_count, 2, QUART, inputs_all)
-    ordered = jnp.take(split_parts, inverse, axis=4)
+    split_parts = received.reshape(items * row_count * 2 * QUART, inputs_all)
+    select = (input_order[:, None] == jnp.arange(inputs_all, dtype=jnp.int32)[None, :]).astype(
+        jnp.bfloat16
+    )
+    ordered = jnp.dot(split_parts, select, preferred_element_type=jnp.float32).astype(jnp.bfloat16)
+    ordered = ordered.reshape(items, row_count, 2, QUART, inputs_all)
     stacked = ordered.reshape(items, row_count * 2 * QUART, inputs_all)
     real_rows = ordered[:, :, 0].reshape(items, row_count * QUART, inputs_all)
     imag_rows = ordered[:, :, 1].reshape(items, row_count * QUART, inputs_all)
@@ -71,6 +216,15 @@
     return packed.astype(jnp.bfloat16)
 
 
+def on_device(samples, fir, chan_assign, input_order):
+    _, frames, slots, frame_len = samples.shape
+    chan_dev = chan_assign.shape[0] // lax.axis_size("chan")
+    whole = slots % 256 == 0 and chan_dev % 16 == 0 and frame_len % 128 == 0
+    whole = whole and fir.shape[0] - 1 <= frames and input_order.shape[0] % 256 == 0
+    form = by_kernels if whole else plain
+    return form(samples, fir, chan_assign, input_order)
+
+
 def solution(mesh):
     in_specs = (P(("grp", "chan"), None, None, None), P(), P(), P())
     out_specs = P(("grp", "chan"), None, None)

time: 714 us -> 262 us (0.37)
  local copies, waits for them, and re-layouts: 255 us -> 1.07 us
  matrix products: 97.2 us -> 0 us
  other arithmetic: 96.1 us -> 6.69 us
  waiting for transfers between devices: 249 us -> 174 us
  Pallas kernels: 0 us -> 71.2 us
    ppermute x1 -> x0, waiting for transfers between devices: 163 us -> none  [shifted(): lax.ppermute(value, axis, [(source, source + steps) for source in range(i...]
    dot_general x3 -> x0, matrix products: 97.2 us -> none  [the longest x1 64.2 us: on_device(): jnp.einsum('kra,krb->kab', stacked, stacked, preferred_element_type=jnp.f...]
    all_to_all x1, waiting for transfers between devices: 86.1 us -> 174 us  [by_kernels(): lax.all_to_all(spectra, 'chan', split_axis=0, concat_axis=0, tiled=True)]
    slice x5 -> x0, local copies, waits for them, and re-layouts: 74.5 us -> none  [the longest x2 47.1 us: on_device(): imag_rows = ordered[:, :, 1].reshape(items, row_count * QUART, inputs_all)]
    gather x2 -> x0, local copies, waits for them, and re-layouts: 72.4 us -> none  [on_device(): ordered = jnp.take(split_parts, inverse, axis=4)]
    pallas_call x0 -> x2, Pallas kernels: none -> 71.2 us  [the longest x1 41.1 us: form_spectra(): pl.pallas_call(spectra_kernel, out_shape=jax.ShapeDtypeStruct((dests, out...]
    dot_general x1 -> x0, local copies, waits for them, and re-layouts: 62.8 us -> none  [on_device(): jnp.einsum('kra,krb->kab', real_rows, imag_rows, preferred_element_type=j...]
    dot_general x1 -> x0, other arithmetic: 58.6 us -> none  [on_device(): jnp.einsum('pcn,fin->cfpi', dft_table, filtered, preferred_element_type=j...]
  transfers between devices with their start and end apart: 2 -> 1, of which waited for: 2 -> 1; matrix products, arithmetic and copies ran while one was open for 2% -> 0% of each run, Pallas kernels for 0% -> 0%
where the time goes in v1:
time: 262 us; the launch traced here: 259 us
  waiting for transfers between devices  174 us (66%)
  Pallas kernels  71.2 us (27%)
  other arithmetic  6.69 us (3%)
  starting transfers between devices  6.41 us (2%)
    all_to_all x1, waiting for transfers between devices, by_kernels(): lax.all_to_all(spectra, 'chan', split_axis=0, concat_axis=0, tiled=True)  174 us
    pallas_call x1, Pallas kernels, form_spectra(): pl.pallas_call(spectra_kernel, out_shape=jax.ShapeDtypeStruct((dests, out...  41.1 us
    pallas_call x1, Pallas kernels, correlate(): pl.pallas_call(correlate_kernel, grid=(chan_dev,), out_shape=jax.ShapeDty...  30.1 us
    all_to_all x1, starting transfers between devices, by_kernels(): lax.all_to_all(spectra, 'chan', split_axis=0, concat_axis=0, tiled=True)  6.41 us
    another operation x1, other arithmetic  5.63 us
  transfers between devices with their start and end apart: 1, of which 1 were waited for; matrix products, arithmetic and copies ran while one was open for 0% of the time, Pallas kernels for 0%

profile of v1, /device:TPU:8, one launch (start us, length us, event | category | flops | bytes accessed | tf_op | source)
XLA Modules:
  0.0 259.4 jit_solution(11154983964683408626)
XLA Ops:
  0.0 5.6 %multiply_convert_fusion.1 = (bf16[1,256,1024]{2,1,0:T(8,128)(2,1)S(1)}, bf16[1,256,1024]{2,1,0:T(8,128)(2,1)S(1)}) fusion(s32[256]{0:T(256)} %param.6), kind=kLoop, calls=%fused_computation.8 | loop fusion | flops 4980736 | bytes 1049600 | tf_op jit(solution)/shard_map/convert
  5.6 1.1 pad_maximum_fusion
  6.7 41.1 %form_spectra.1 = bf16[16,31,2,16,256]{4,3,2,1,0:T(8,128)(2,1)} custom-call(bf16[16,256,1024]{2,1,0:T(8,128)(2,1)} %bitcast.3, f32[16,1024]{1,0:T(8,128)} %fir_ref.1, bf16[512,1024]{1,0:T(8,128)(2,1)} %bitcast.4), custom_call_target="tpu_custom_call" | custom-call | tf_op jit(solution)/shard_map/form_spectra/pallas_call | solution.py:68
  47.8 0.0 copy-start
  47.8 6.4 %all-to-all-start = ((bf16[16,31,2,16,256]{4,3,2,1,0:T(8,128)(2,1)}), bf16[16,31,2,16,256]{4,3,2,1,0:T(8,128)(2,1)}, u32[]{:S(2)}, u32[]{:S(2)}) async-start(bf16[16,31,2,16,256]{4,3,2,1,0:T(8,128)(2,1)} %form_spectra.1), calls=%async_computation | async-start | bytes 16252928 | tf_op jit(solution)/shard_map/all_to_all | solution.py:166
  54.2 0.0 copy-done
  54.2 1.1 copy.5.order_ref
  55.3 174.0 %all-to-all-done.spec_ref = bf16[16,31,2,16,256]{4,3,2,1,0:T(8,128)(2,1)} async-done(((bf16[16,31,2,16,256]{4,3,2,1,0:T(8,128)(2,1)}), bf16[16,31,2,16,256]{4,3,2,1,0:T(8,128)(2,1)}, u32[]{:S(2)}, u32[]{:S(2)}) %all-to-all-start) | async-done | bytes 8126496 | tf_op jit(solution)/shard_map/all_to_all | solution.py:166
  229.3 30.1 %correlate.1 = bf16[16,1024,1024]{2,1,0:T(8,128)(2,1)} custom-call(bf16[16,31,2,16,256]{4,3,2,1,0:T(8,128)(2,1)} %all-to-all-done.spec_ref, s32[1024,1]{1,0:T(8,128)} %copy.5.order_ref), custom_call_target="tpu_custom_call" | custom-call | tf_op jit(solution)/shard_map/correlate/pallas_call | solution.py:144
Async XLA Ops:
  47.8 6.4 %copy-start = (s32[1024]{0:T(1024)S(1)}, s32[1024]{0:T(1024)}, u32[]{:S(2)}) copy-start(s32[1024]{0:T(1024)} %param.7) | copy-start | bytes 12292
  47.8 181.5 %all-to-all-start = ((bf16[16,31,2,16,256]{4,3,2,1,0:T(8,128)(2,1)}), bf16[16,31,2,16,256]{4,3,2,1,0:T(8,128)(2,1)}, u32[]{:S(2)}, u32[]{:S(2)}) async-start(bf16[16,31,2,16,256]{4,3,2,1,0:T(8,128)(2,1)} %form_spectra.1), calls=%async_computation | async-start | bytes 16252928 | tf_op jit(solution)/shard_map/all_to_all | solution.py:166

commit v2 on v1

--- a/solution.py
+++ b/solution.py
@@ -76,6 +76,160 @@
     )(own_frames, fir, dft_table.reshape(-1, frame_len))
 
 
+def exchange_kernel(
+    spec_ref, recv_ref, merged, own_send, own_recv, tail_send, tail_recv, lead_send, lead_recv, local
+):
+    dests, outs, _, _, _ = spec_ref.shape
+    frames = merged.shape[1]
+    lead = outs - frames
+    groups = dests // QUART
+    me = lax.axis_index("chan")
+    quarter = lax.div(me, groups)
+    after = lax.rem(me + groups, dests)
+    part = lax.axis_index("grp")
+    head, tail = pl.ds(0, frames), pl.ds(frames, lead)
+
+    def remote(src, dst, send, recv, device):
+        return pltpu.make_async_remote_copy(
+            src_ref=src,
+            dst_ref=dst,
+            send_sem=send,
+            recv_sem=recv,
+            device_id=(part, device),
+            device_id_type=pl.DeviceIdType.MESH,
+        )
+
+    def send_own(d):
+        return remote(
+            spec_ref.at[d, head], recv_ref.at[me, head], own_send.at[d], own_recv.at[me], d
+        )
+
+    def send_merged(d):
+        return remote(merged.at[d], recv_ref.at[me, head], own_send.at[d], own_recv.at[me], d)
+
+    def send_tail(d):
+        return remote(
+            spec_ref.at[d, tail], recv_ref.at[me, tail], tail_send.at[d], tail_recv.at[me], d
+        )
+
+    def send_lead(d):
+        return remote(
+            spec_ref.at[d, tail],
+            merged.at[d, pl.ds(0, lead)],
+            lead_send.at[d],
+            lead_recv.at[d],
+            after,
+        )
+
+    barrier = pltpu.get_barrier_semaphore()
+
+    @pl.loop(1, dests)
+    def _(k):
+        other = lax.rem(me + k, dests)
+        pl.semaphore_signal(
+            barrier, inc=1, device_id=(part, other), device_id_type=pl.DeviceIdType.MESH
+        )
+
+    pl.semaphore_wait(barrier, dests - 1)
+    has_tail = quarter < QUART - 1
+    stay = pltpu.make_async_copy(spec_ref.at[me], recv_ref.at[me], local)
+
+    @pl.loop(0, dests)
+    def _(d):
+        @pl.when(quarter < lax.div(d, groups) - 1)
+        def _():
+            send_lead(d).start()
+
+    @pl.loop(1, dests)
+    def _(k):
+        d = lax.rem(me + k, dests)
+
+        @pl.when(quarter >= lax.div(d, groups))
+        def _():
+            send_own(d).start()
+
+            @pl.when(has_tail)
+            def _():
+                send_tail(d).start()
+
+    stay.start()
+
+    @pl.loop(0, dests)
+    def _(d):
+        @pl.when(quarter < lax.div(d, groups) - 1)
+        def _():
+            send_lead(d).wait_send()
+
+    @pl.loop(1, dests)
+    def _(k):
+        d = lax.rem(me + dests - k, dests)
+        target = lax.div(d, groups)
+
+        @pl.when((quarter == 0) & (target > 0))
+        def _():
+            send_own(d).start()
+
+        @pl.when(quarter == target - 1)
+        def _():
+            send_tail(d).start()
+
+    @pl.loop(0, dests)
+    def _(d):
+        @pl.when((quarter >= 1) & (quarter < lax.div(d, groups)))
+        def _():
+            send_lead(d).wait_recv()
+
+            @pl.loop(0, lead)
+            def _(f):
+                merged[d, f] = (
+                    merged[d, f].astype(jnp.float32) + spec_ref[d, f].astype(jnp.float32)
+                ).astype(jnp.bfloat16)
+
+            for f in range(lead, frames):
+                merged[d, f] = spec_ref[d, f]
+            send_merged(d).start()
+
+    stay.wait()
+
+    @pl.loop(1, dests)
+    def _(k):
+        d = lax.rem(me + k, dests)
+        target = lax.div(d, groups)
+        send_own(d).wait_send()
+
+        @pl.when(has_tail & (quarter >= target - 1))
+        def _():
+            send_tail(d).wait_send()
+
+        remote(
+            spec_ref.at[d, head], recv_ref.at[d, head], own_send.at[d], own_recv.at[d], d
+        ).wait_recv()
+
+        @pl.when((target < QUART - 1) & (target >= quarter - 1))
+        def _():
+            remote(
+                spec_ref.at[d, tail], recv_ref.at[d, tail], tail_send.at[d], tail_recv.at[d], d
+            ).wait_recv()
+
+
+def exchange(spectra, frames):
+    dests, outs, two, chan_dev, slots = spectra.shape
+    copies = pltpu.SemaphoreType.DMA((dests,))
+    return pl.pallas_call(
+        exchange_kernel,
+        out_shape=jax.ShapeDtypeStruct(spectra.shape, spectra.dtype),
+        in_specs=[pl.BlockSpec(memory_space=pltpu.VMEM)],
+        out_specs=pl.BlockSpec(memory_space=pl.ANY),
+        scratch_shapes=[pltpu.VMEM((dests, frames, two, chan_dev, slots), spectra.dtype)]
+        + [copies] * 6
+        + [pltpu.SemaphoreType.DMA],
+        compiler_params=pltpu.CompilerParams(
+            collective_id=0, has_side_effects=True, vmem_limit_bytes=VMEM
+        ),
+        name="exchange",
+    )(spectra)
+
+
 def correlate_kernel(spec_ref, order_ref, out_ref, gathered, select, ordered):
     sources, outs, _, chan_dev, slots = spec_ref.shape
     groups = sources // QUART
@@ -85,22 +239,29 @@
     lead = outs - frames
     spectra_total = QUART * frames
 
+    quarter = lax.div(lax.axis_index("chan"), groups)
+
+    def gather(q, add):
+        for p in range(2):
+            base = (p * QUART + q) * frames * chan_dev
+            for g in range(groups):
+                cols = slice(g * slots, (g + 1) * slots)
+                source = q * groups + g
+                for f in range(frames):
+                    value = spec_ref[source, f, p]
+                    if add and f < lead:
+                        value = (
+                            value.astype(jnp.float32)
+                            + spec_ref[source - groups, frames + f, p].astype(jnp.float32)
+                        ).astype(jnp.bfloat16)
+                    gathered[base + f * chan_dev : base + (f + 1) * chan_dev, cols] = value
+
     @pl.when(pl.program_id(0) == 0)
     def _():
-        for p in range(2):
-            for q in range(QUART):
-                base = (p * QUART + q) * frames * chan_dev
-                for g in range(groups):
-                    cols = slice(g * slots, (g + 1) * slots)
-                    source = q * groups + g
-                    for f in range(frames):
-                        value = spec_ref[source, f, p]
-                        if q > 0 and f < lead:
-                            value = (
-                                value.astype(jnp.float32)
-                                + spec_ref[source - groups, frames + f, p].astype(jnp.float32)
-                            ).astype(jnp.bfloat16)
-                        gathered[base + f * chan_dev : base + (f + 1) * chan_dev, cols] = value
+        gather(0, False)
+        for q in range(1, QUART):
+            pl.when(q >= quarter)(lambda q=q: gather(q, True))
+            pl.when(q < quarter)(lambda q=q: gather(q, False))
         for begin in range(0, inputs, 128):
             names = lax.broadcasted_iota(jnp.int32, (128, inputs), 1)
             hit = names == order_ref[begin : begin + 128, :]
@@ -163,7 +324,7 @@
     chan_count = lax.axis_size("chan")
     dft_table = make_table(chan_assign, frame_len)
     spectra = form_spectra(own_frames, fir, dft_table, chan_count)
-    received = lax.all_to_all(spectra, "chan", split_axis=0, concat_axis=0, tiled=True)
+    received = exchange(spectra, frames)
     return correlate(received, input_order, frames)
 
 

time: 262 us -> 223 us (0.85)
  waiting for transfers between devices: 174 us -> 0 us
  Pallas kernels: 71.2 us -> 213 us
  starting transfers between devices: 6.41 us -> 0 us
    all_to_all x1 -> x0, waiting for transfers between devices: 174 us -> none  [by_kernels(): lax.all_to_all(spectra, 'chan', split_axis=0, concat_axis=0, tiled=True)]
    pallas_call x0 -> x1, Pallas kernels: none -> 142 us  [exchange(): pl.pallas_call(exchange_kernel, out_shape=jax.ShapeDtypeStruct(spectra.sh...]
    all_to_all x1 -> x0, starting transfers between devices: 6.41 us -> none  [by_kernels(): lax.all_to_all(spectra, 'chan', split_axis=0, concat_axis=0, tiled=True)]
  transfers between devices with their start and end apart: 1 -> 0, of which waited for: 1 -> 0; matrix products, arithmetic and copies ran while one was open for 0% -> 0% of each run, Pallas kernels for 0% -> 0%
where the time goes in v2:
time: 223 us; the launch traced here: 222 us
  Pallas kernels  213 us (96%)
  other arithmetic  6.71 us (3%)
    pallas_call x1, Pallas kernels, exchange(): pl.pallas_call(exchange_kernel, out_shape=jax.ShapeDtypeStruct(spectra.sh...  142 us
    pallas_call x1, Pallas kernels, form_spectra(): pl.pallas_call(spectra_kernel, out_shape=jax.ShapeDtypeStruct((dests, out...  41 us
    pallas_call x1, Pallas kernels, correlate(): pl.pallas_call(correlate_kernel, grid=(chan_dev,), out_shape=jax.ShapeDty...  30.2 us
    another operation x1, other arithmetic  5.63 us

profile of v2, /device:TPU:8, one launch (start us, length us, event | category | flops | bytes accessed | tf_op | source)
XLA Modules:
  0.0 221.8 jit_solution(10319457788266955405)
XLA Ops:
  0.0 1.8 copy.5.order_ref
  1.8 5.6 %multiply_convert_fusion.1 = (bf16[1,256,1024]{2,1,0:T(8,128)(2,1)S(1)}, bf16[1,256,1024]{2,1,0:T(8,128)(2,1)S(1)}) fusion(s32[256]{0:T(256)} %param.6), kind=kLoop, calls=%fused_computation.8 | loop fusion | flops 4980736 | bytes 1049600 | tf_op jit(solution)/shard_map/convert
  7.4 1.1 pad_maximum_fusion
  8.5 41.0 %form_spectra.1.spec_ref = bf16[16,31,2,16,256]{4,3,2,1,0:T(8,128)(2,1)} custom-call(bf16[16,256,1024]{2,1,0:T(8,128)(2,1)} %bitcast.3, f32[16,1024]{1,0:T(8,128)} %fir_ref.1, bf16[512,1024]{1,0:T(8,128)(2,1)} %bitcast.4), custom_call_target="tpu_custom_call" | custom-call | tf_op jit(solution)/shard_map/form_spectra/pallas_call | solution.py:68
  49.5 142.1 %exchange.1.spec_ref = bf16[16,31,2,16,256]{4,3,2,1,0:T(8,128)(2,1)} custom-call(bf16[16,31,2,16,256]{4,3,2,1,0:T(8,128)(2,1)} %form_spectra.1.spec_ref), custom_call_target="tpu_custom_call" | custom-call | tf_op jit(solution)/shard_map/exchange/pallas_call | solution.py:218
  191.5 30.2 %correlate.1 = bf16[16,1024,1024]{2,1,0:T(8,128)(2,1)} custom-call(bf16[16,31,2,16,256]{4,3,2,1,0:T(8,128)(2,1)} %exchange.1.spec_ref, s32[1024,1]{1,0:T(8,128)} %copy.5.order_ref), custom_call_target="tpu_custom_call" | custom-call | tf_op jit(solution)/shard_map/correlate/pallas_call | solution.py:305

commit v3 on v2

--- a/solution.py
+++ b/solution.py
@@ -27,10 +27,34 @@
     )
 
 
-def spectra_kernel(x_ref, fir_ref, dft_ref, out_ref, filt):
+def phase_parts(chan_assign, frame_len):
+    def turn(steps):
+        phase = chan_assign[:, None] * steps[None, :] % frame_len
+        angles = phase.astype(jnp.float32) * (2.0 * math.pi / frame_len)
+        return jnp.stack([jnp.cos(angles), jnp.sin(angles)])
+
+    high = turn(128 * jnp.arange(frame_len // 128, dtype=jnp.int32))
+    return high, turn(jnp.arange(128, dtype=jnp.int32))
+
+
+def fill_table(high_ref, low_ref, table):
+    chans = low_ref.shape[1]
+    frame_len = table.shape[1]
+    scale = 1.0 / math.sqrt(frame_len)
+    cos_low, sin_low = low_ref[0], low_ref[1]
+    for h in range(frame_len // 128):
+        cos_high, sin_high = high_ref[0, :, h : h + 1], high_ref[1, :, h : h + 1]
+        cols = slice(h * 128, (h + 1) * 128)
+        real = (cos_high * cos_low - sin_high * sin_low) * scale
+        imag = (sin_high * cos_low + cos_high * sin_low) * -scale
+        table[:chans, cols] = real.astype(jnp.bfloat16)
+        table[chans:, cols] = imag.astype(jnp.bfloat16)
+
+
+def form(x_ref, fir_ref, table, filt, spec_ref, first, count):
     frames, slots, frame_len = x_ref.shape
     taps = fir_ref.shape[0]
-    dests, outs, _, chan_dev, _ = out_ref.shape
+    dests, _, _, chan_dev, _ = spec_ref.shape
     slot_tiles = slots // 16
 
     @pl.loop(0, slot_tiles * (frame_len // 128))
@@ -39,18 +63,18 @@
         cols = pl.ds(pl.multiple_of(lax.div(step, slot_tiles) * 128, 128), 128)
         x = [x_ref[f, rows, cols].astype(jnp.float32) for f in range(frames)]
         fir = [fir_ref[t : t + 1, cols] for t in range(taps)]
-        for o in range(outs):
+        for o in range(first, first + count):
             accum = None
             for t in range(taps):
                 if 0 <= o - t < frames:
                     term = fir[t] * x[o - t]
                     accum = term if accum is None else accum + term
-            filt[o, rows, cols] = accum.astype(jnp.bfloat16)
-
-    @pl.loop(0, outs)
+            filt[o - first, rows, cols] = accum.astype(jnp.bfloat16)
+
+    @pl.loop(0, count)
     def _(o):
         result = lax.dot_general(
-            dft_ref[...],
+            table[...],
             filt[o],
             (((1,), (1,)), ((), ())),
             preferred_element_type=jnp.float32,
@@ -58,26 +82,26 @@
         for p in range(2):
             for d in range(dests):
                 begin = (p * dests + d) * chan_dev
-                out_ref[d, o, p] = result[begin : begin + chan_dev]
-
-
-def form_spectra(own_frames, fir, dft_table, dests):
-    frames, slots, frame_len = own_frames.shape
-    outs = frames + fir.shape[0] - 1
-    chan_dev = dft_table.shape[1] // dests
-    return pl.pallas_call(
-        spectra_kernel,
-        out_shape=jax.ShapeDtypeStruct((dests, outs, 2, chan_dev, slots), jnp.bfloat16),
-        in_specs=[pl.BlockSpec(memory_space=pltpu.VMEM)] * 3,
-        out_specs=pl.BlockSpec(memory_space=pltpu.VMEM),
-        scratch_shapes=[pltpu.VMEM((outs, slots, frame_len), jnp.bfloat16)],
-        compiler_params=pltpu.CompilerParams(vmem_limit_bytes=VMEM),
-        name="form_spectra",
-    )(own_frames, fir, dft_table.reshape(-1, frame_len))
+                spec_ref[d, first + o, p] = result[begin : begin + chan_dev]
 
 
 def exchange_kernel(
-    spec_ref, recv_ref, merged, own_send, own_recv, tail_send, tail_recv, lead_send, lead_recv, local
+    x_ref,
+    fir_ref,
+    high_ref,
+    low_ref,
+    recv_ref,
+    table,
+    filt,
+    spec_ref,
+    merged,
+    own_send,
+    own_recv,
+    tail_send,
+    tail_recv,
+    lead_send,
+    lead_recv,
+    local,
 ):
     dests, outs, _, _, _ = spec_ref.shape
     frames = merged.shape[1]
@@ -132,13 +156,31 @@
 
     pl.semaphore_wait(barrier, dests - 1)
     has_tail = quarter < QUART - 1
-    stay = pltpu.make_async_copy(spec_ref.at[me], recv_ref.at[me], local)
-
-    @pl.loop(0, dests)
-    def _(d):
-        @pl.when(quarter < lax.div(d, groups) - 1)
-        def _():
-            send_lead(d).start()
+    no_lead = quarter >= QUART - 2
+    stay = pltpu.make_async_copy(spec_ref.at[me, head], recv_ref.at[me, head], local.at[0])
+    stay_tail = pltpu.make_async_copy(spec_ref.at[me, tail], recv_ref.at[me, tail], local.at[1])
+    fill_table(high_ref, low_ref, table)
+
+    @pl.when(has_tail)
+    def _():
+        form(x_ref, fir_ref, table, filt, spec_ref, frames, lead)
+        stay_tail.start()
+
+        @pl.loop(0, dests)
+        def _(d):
+            @pl.when(quarter < lax.div(d, groups) - 1)
+            def _():
+                send_lead(d).start()
+
+        @pl.loop(1, dests)
+        def _(k):
+            d = lax.rem(me + k, dests)
+
+            @pl.when(no_lead | (quarter >= lax.div(d, groups)))
+            def _():
+                send_tail(d).start()
+
+    form(x_ref, fir_ref, table, filt, spec_ref, 0, frames)
 
     @pl.loop(1, dests)
     def _(k):
@@ -147,10 +189,6 @@
         @pl.when(quarter >= lax.div(d, groups))
         def _():
             send_own(d).start()
-
-            @pl.when(has_tail)
-            def _():
-                send_tail(d).start()
 
     stay.start()
 
@@ -169,7 +207,7 @@
         def _():
             send_own(d).start()
 
-        @pl.when(quarter == target - 1)
+        @pl.when((quarter < QUART - 2) & (quarter == target - 1))
         def _():
             send_tail(d).start()
 
@@ -190,6 +228,7 @@
             send_merged(d).start()
 
     stay.wait()
+    pl.when(has_tail)(stay_tail.wait)
 
     @pl.loop(1, dests)
     def _(k):
@@ -212,22 +251,31 @@
             ).wait_recv()
 
 
-def exchange(spectra, frames):
-    dests, outs, two, chan_dev, slots = spectra.shape
+def exchange(own_frames, fir, high, low, dests):
+    frames, slots, frame_len = own_frames.shape
+    lead = fir.shape[0] - 1
+    chans = low.shape[1]
+    chan_dev = chans // dests
+    spectra = (dests, frames + lead, 2, chan_dev, slots)
     copies = pltpu.SemaphoreType.DMA((dests,))
     return pl.pallas_call(
         exchange_kernel,
-        out_shape=jax.ShapeDtypeStruct(spectra.shape, spectra.dtype),
-        in_specs=[pl.BlockSpec(memory_space=pltpu.VMEM)],
+        out_shape=jax.ShapeDtypeStruct(spectra, jnp.bfloat16),
+        in_specs=[pl.BlockSpec(memory_space=pltpu.VMEM)] * 4,
         out_specs=pl.BlockSpec(memory_space=pl.ANY),
-        scratch_shapes=[pltpu.VMEM((dests, frames, two, chan_dev, slots), spectra.dtype)]
+        scratch_shapes=[
+            pltpu.VMEM((2 * chans, frame_len), jnp.bfloat16),
+            pltpu.VMEM((frames, slots, frame_len), jnp.bfloat16),
+            pltpu.VMEM(spectra, jnp.bfloat16),
+            pltpu.VMEM((dests, frames, 2, chan_dev, slots), jnp.bfloat16),
+        ]
         + [copies] * 6
-        + [pltpu.SemaphoreType.DMA],
+        + [pltpu.SemaphoreType.DMA((2,))],
         compiler_params=pltpu.CompilerParams(
             collective_id=0, has_side_effects=True, vmem_limit_bytes=VMEM
         ),
         name="exchange",
-    )(spectra)
+    )(own_frames, fir, high, low)
 
 
 def correlate_kernel(spec_ref, order_ref, out_ref, gathered, select, ordered):
@@ -322,9 +370,8 @@
     own_frames = samples[0]
     frames, _, frame_len = own_frames.shape
     chan_count = lax.axis_size("chan")
-    dft_table = make_table(chan_assign, frame_len)
-    spectra = form_spectra(own_frames, fir, dft_table, chan_count)
-    received = exchange(spectra, frames)
+    high, low = phase_parts(chan_assign, frame_len)
+    received = exchange(own_frames, fir, high, low, chan_count)
     return correlate(received, input_order, frames)
 
 

time: 223 us -> 206 us (0.924)
  Pallas kernels: 213 us -> 201 us
  other arithmetic: 6.71 us -> 2.79 us
    pallas_call x2 -> x1, Pallas kernels: 183 us -> 170 us  [exchange(): pl.pallas_call(exchange_kernel, out_shape=jax.ShapeDtypeStruct(spectra, j...]
    another operation x2, other arithmetic: 6.71 us -> 0.72 us  [turn(): return jnp.stack([jnp.cos(angles), jnp.sin(angles)])]
where the time goes in v3:
time: 206 us
  Pallas kernels  201 us (98%)
  other arithmetic  2.79 us (1%)
  local copies, waits for them, and re-layouts  2.6 us (1%)
    pallas_call x1, Pallas kernels, exchange(): pl.pallas_call(exchange_kernel, out_shape=jax.ShapeDtypeStruct(spectra, j...  170 us
    pallas_call x1, Pallas kernels, correlate(): pl.pallas_call(correlate_kernel, grid=(chan_dev,), out_shape=jax.ShapeDty...  30.2 us

profile of v3, /device:TPU:8, one launch (start us, length us, event | category | flops | bytes accessed | tf_op | source)
XLA Modules:
  0.0 206.1 jit_solution(11043951543169427224)
XLA Ops:
  0.0 0.8 fusion.12
  0.8 0.8 copy.6.high_ref
  1.7 1.3 fusion.7
  2.9 0.7 pad_maximum_fusion.low_ref
  3.6 1.8 copy.7.order_ref
  5.4 170.5 %exchange.1.spec_ref = bf16[16,31,2,16,256]{4,3,2,1,0:T(8,128)(2,1)} custom-call(bf16[16,256,1024]{2,1,0:T(8,128)(2,1)} %bitcast.2, f32[16,1024]{1,0:T(8,128)} %fir_ref.1, f32[2,256,8]{2,1,0:T(8,128)} %copy.6.high_ref, f32[2,256,128]{2,1,0:T(8,128)} %pad_maximum_fusion.low_ref), custom_call_target="tpu_custom_call" | custom-call | tf_op jit(solution)/shard_map/exchange/pallas_call | solution.py:261
  175.9 30.2 %correlate.1 = bf16[16,1024,1024]{2,1,0:T(8,128)(2,1)} custom-call(bf16[16,31,2,16,256]{4,3,2,1,0:T(8,128)(2,1)} %exchange.1.spec_ref, s32[1024,1]{1,0:T(8,128)} %copy.7.order_ref), custom_call_target="tpu_custom_call" | custom-call | tf_op jit(solution)/shard_map/correlate/pallas_call | solution.py:353
  (2 shorter events, 0.0 us)

commit v4 on v3

--- a/solution.py
+++ b/solution.py
@@ -112,6 +112,8 @@
     after = lax.rem(me + groups, dests)
     part = lax.axis_index("grp")
     head, tail = pl.ds(0, frames), pl.ds(frames, lead)
+    split = (lead + 1) // 2
+    parts = ((split, lead - split), (0, split))
 
     def remote(src, dst, send, recv, device):
         return pltpu.make_async_remote_copy(
@@ -131,17 +133,23 @@
     def send_merged(d):
         return remote(merged.at[d], recv_ref.at[me, head], own_send.at[d], own_recv.at[me], d)
 
-    def send_tail(d):
+    def send_tail(d, h):
+        here = pl.ds(frames + parts[h][0], parts[h][1])
         return remote(
-            spec_ref.at[d, tail], recv_ref.at[me, tail], tail_send.at[d], tail_recv.at[me], d
+            spec_ref.at[d, here],
+            recv_ref.at[me, here],
+            tail_send.at[h, d],
+            tail_recv.at[h, me],
+            d,
         )
 
-    def send_lead(d):
+    def send_lead(d, h):
+        begin, count = parts[h]
         return remote(
-            spec_ref.at[d, tail],
-            merged.at[d, pl.ds(0, lead)],
-            lead_send.at[d],
-            lead_recv.at[d],
+            spec_ref.at[d, pl.ds(frames + begin, count)],
+            merged.at[d, pl.ds(begin, count)],
+            lead_send.at[h, d],
+            lead_recv.at[h, d],
             after,
         )
 
@@ -163,22 +171,24 @@
 
     @pl.when(has_tail)
     def _():
-        form(x_ref, fir_ref, table, filt, spec_ref, frames, lead)
+        for h in range(2):
+            form(x_ref, fir_ref, table, filt, spec_ref, frames + parts[h][0], parts[h][1])
+
+            @pl.loop(0, dests)
+            def _(d):
+                @pl.when(quarter < lax.div(d, groups) - 1)
+                def _():
+                    send_lead(d, h).start()
+
+            @pl.loop(1, dests)
+            def _(k):
+                d = lax.rem(me + k, dests)
+
+                @pl.when(no_lead | (quarter >= lax.div(d, groups)))
+                def _():
+                    send_tail(d, h).start()
+
         stay_tail.start()
-
-        @pl.loop(0, dests)
-        def _(d):
-            @pl.when(quarter < lax.div(d, groups) - 1)
-            def _():
-                send_lead(d).start()
-
-        @pl.loop(1, dests)
-        def _(k):
-            d = lax.rem(me + k, dests)
-
-            @pl.when(no_lead | (quarter >= lax.div(d, groups)))
-            def _():
-                send_tail(d).start()
 
     form(x_ref, fir_ref, table, filt, spec_ref, 0, frames)
 
@@ -196,7 +206,8 @@
     def _(d):
         @pl.when(quarter < lax.div(d, groups) - 1)
         def _():
-            send_lead(d).wait_send()
+            send_lead(d, 0).wait_send()
+            send_lead(d, 1).wait_send()
 
     @pl.loop(1, dests)
     def _(k):
@@ -209,13 +220,15 @@
 
         @pl.when((quarter < QUART - 2) & (quarter == target - 1))
         def _():
-            send_tail(d).start()
+            send_tail(d, 0).start()
+            send_tail(d, 1).start()
 
     @pl.loop(0, dests)
     def _(d):
         @pl.when((quarter >= 1) & (quarter < lax.div(d, groups)))
         def _():
-            send_lead(d).wait_recv()
+            send_lead(d, 0).wait_recv()
+            send_lead(d, 1).wait_recv()
 
             @pl.loop(0, lead)
             def _(f):
@@ -238,7 +251,8 @@
 
         @pl.when(has_tail & (quarter >= target - 1))
         def _():
-            send_tail(d).wait_send()
+            send_tail(d, 0).wait_send()
+            send_tail(d, 1).wait_send()
 
         remote(
             spec_ref.at[d, head], recv_ref.at[d, head], own_send.at[d], own_recv.at[d], d
@@ -246,9 +260,15 @@
 
         @pl.when((target < QUART - 1) & (target >= quarter - 1))
         def _():
-            remote(
-                spec_ref.at[d, tail], recv_ref.at[d, tail], tail_send.at[d], tail_recv.at[d], d
-            ).wait_recv()
+            for h in range(2):
+                here = pl.ds(frames + parts[h][0], parts[h][1])
+                remote(
+                    spec_ref.at[d, here],
+                    recv_ref.at[d, here],
+                    tail_send.at[h, d],
+                    tail_recv.at[h, d],
+                    d,
+                ).wait_recv()
 
 
 def exchange(own_frames, fir, high, low, dests):
@@ -269,7 +289,8 @@
             pltpu.VMEM(spectra, jnp.bfloat16),
             pltpu.VMEM((dests, frames, 2, chan_dev, slots), jnp.bfloat16),
         ]
-        + [copies] * 6
+        + [copies] * 2
+        + [pltpu.SemaphoreType.DMA((2, dests))] * 4
         + [pltpu.SemaphoreType.DMA((2,))],
         compiler_params=pltpu.CompilerParams(
             collective_id=0, has_side_effects=True, vmem_limit_bytes=VMEM

time: 206 us -> 204 us (level)
  Pallas kernels: 201 us -> 198 us
    pallas_call x1, Pallas kernels: 170 us -> 168 us  [exchange(): pl.pallas_call(exchange_kernel, out_shape=jax.ShapeDtypeStruct(spectra, j...]
where the time goes in v4:
time: 204 us; the launch traced here: 203 us
  Pallas kernels  198 us (97%)
  other arithmetic  2.79 us (1%)
  local copies, waits for them, and re-layouts  2.6 us (1%)
    pallas_call x1, Pallas kernels, exchange(): pl.pallas_call(exchange_kernel, out_shape=jax.ShapeDtypeStruct(spectra, j...  168 us
    pallas_call x1, Pallas kernels, correlate(): pl.pallas_call(correlate_kernel, grid=(chan_dev,), out_shape=jax.ShapeDty...  30.2 us

profile of v4, /device:TPU:8, one launch (start us, length us, event | category | flops | bytes accessed | tf_op | source)
XLA Modules:
  0.0 203.2 jit_solution(1321426768400020468)
XLA Ops:
  0.0 0.8 fusion.12
  0.8 0.8 copy.6.high_ref
  1.7 1.3 fusion.7
  2.9 0.7 pad_maximum_fusion.low_ref
  3.6 1.8 copy.7.order_ref
  5.4 167.6 %exchange.1.spec_ref = bf16[16,31,2,16,256]{4,3,2,1,0:T(8,128)(2,1)} custom-call(bf16[16,256,1024]{2,1,0:T(8,128)(2,1)} %bitcast.2, f32[16,1024]{1,0:T(8,128)} %fir_ref.1, f32[2,256,8]{2,1,0:T(8,128)} %copy.6.high_ref, f32[2,256,128]{2,1,0:T(8,128)} %pad_maximum_fusion.low_ref), custom_call_target="tpu_custom_call" | custom-call | tf_op jit(solution)/shard_map/exchange/pallas_call | solution.py:281
  173.0 30.2 %correlate.1 = bf16[16,1024,1024]{2,1,0:T(8,128)(2,1)} custom-call(bf16[16,31,2,16,256]{4,3,2,1,0:T(8,128)(2,1)} %exchange.1.spec_ref, s32[1024,1]{1,0:T(8,128)} %copy.7.order_ref), custom_call_target="tpu_custom_call" | custom-call | tf_op jit(solution)/shard_map/correlate/pallas_call | solution.py:374
  (2 shorter events, 0.0 us)
